TPU v7x, 512 devices: a whole 4x4x16 slice. The times are simulated.
512 devices in a mesh: dp: 128 (over z, x, core), mp: 4 (over y).
Axes of the slice: x: 4, y: 4, z: 16, core: 2. Of those that a mesh axis runs over, the one named last changes fastest.
Arguments:
- states: bfloat16 [32768, 2048], P('dp'), may hold values from -6 to 6
- inner_weights: bfloat16 [2, 2048, 3072], P(None, 'dp', 'mp'), may hold values from -0.125 to 0.125
- down_weight: bfloat16 [1024, 3072], P('dp', 'mp'), may hold values from -0.109375 to 0.109375
- cotangent: bfloat16 [32768, 1024], P('dp'), may hold values from -24 to 24
- routes: int32 [32768], P('dp'), may hold values from -1 to 127, as said below
Outputs:
- layer_output: bfloat16 [32768, 1024], P('dp', 'mp')
- grad_gates: bfloat16 [32768, 3072], P('dp', 'mp')
- grad_linear: bfloat16 [32768, 3072], P('dp', 'mp')
- down_grad: float32 [1024, 3072], P('dp', 'mp')
Inputs may be any that keep to these rules, and one draw needn't show every extreme that they name: `routes`: -1 marks a dropped token; otherwise the data-axis index of the device that takes its row. Among the 256 rows of one data-axis index at most 2 kept rows name any one destination; one destination is named by exactly 2 kept rows of every index; every index keeps 2 rows or more.
All inputs are finite; a program needn't handle non-finite values.
Results may differ from a plain program's by a relative error of at most 0.013.
Values may be sent and summed in bfloat16 or wider, within the bound.
A program may use at most 64 MiB of HBM per device.

v0:
```python
import jax
import jax.numpy as jnp
from jax import lax
from jax.sharding import PartitionSpec as P


def activations(gate_pre, up_pre):
    gate_float = gate_pre.astype(jnp.float32)
    up_float = up_pre.astype(jnp.float32)
    sigmoid_gate = jax.nn.sigmoid(gate_float)
    active = gate_float * sigmoid_gate
    hidden = (active * up_float).astype(jnp.bfloat16)
    return (gate_float, up_float, sigmoid_gate, active, hidden)


def gate_grads(d_hidden, gate_float, up_float, sigmoid_gate, active):
    grad_gate = (
        d_hidden * up_float * (sigmoid_gate * (1.0 + gate_float * (1.0 - sigmoid_gate)))
    ).astype(jnp.bfloat16)
    grad_up = (d_hidden * active).astype(jnp.bfloat16)
    return jnp.concatenate([grad_gate, grad_up], axis=1)


def body(states, inner_weights, down_weight, cotangent, routes):
    inner_full, down_full = (
        lax.all_gather(inner_weights, "dp", axis=1, tiled=True),
        lax.all_gather(down_weight, "dp", axis=0, tiled=True),
    )
    gate_pre = jnp.dot(states, inner_full[0], preferred_element_type=jnp.float32).astype(
        jnp.bfloat16
    )
    up_pre = jnp.dot(states, inner_full[1], preferred_element_type=jnp.float32).astype(jnp.bfloat16)
    gate_float, up_float, sigmoid_gate, active, hidden = activations(gate_pre, up_pre)
    partial_value = lax.dot_general(
        hidden, down_full, (((1,), (1,)), ((), ())), preferred_element_type=jnp.float32
    )
    layer_output = lax.psum_scatter(
        partial_value.astype(jnp.bfloat16), "mp", scatter_dimension=1, tiled=True
    )
    tok_rows = states.shape[0]
    kept_rows = routes >= 0
    zero_value = jnp.zeros((), jnp.bfloat16)
    kept_cot = jnp.where(kept_rows[:, None], cotangent, zero_value)
    shards = lax.axis_size("dp")
    capacity = max(2, tok_rows // shards)
    slot_total = shards * capacity
    targets = jnp.arange(shards, dtype=jnp.int32)
    onehot = (routes[:, None] == targets[None, :]).astype(jnp.int32)
    earlier = jnp.cumsum(onehot, axis=0) - onehot
    slot_index = jnp.sum(earlier * onehot, axis=1)
    flat_index = jnp.where(kept_rows, routes * capacity + slot_index, slot_total)
    preacts = jnp.concatenate([gate_pre, up_pre], axis=1)
    send_acts = (
        jnp.zeros((slot_total + 1, preacts.shape[1]), jnp.bfloat16)
        .at[flat_index]
        .set(preacts)[:slot_total]
    )
    send_cot = (
        jnp.zeros((slot_total + 1, kept_cot.shape[1]), jnp.bfloat16)
        .at[flat_index]
        .set(kept_cot)[:slot_total]
    )
    recv_acts, recv_cot = (
        lax.all_to_all(
            send_acts.reshape(shards, capacity, -1), "dp", split_axis=0, concat_axis=0, tiled=True
        ),
        lax.all_to_all(
            send_cot.reshape(shards, capacity, -1), "dp", split_axis=0, concat_axis=0, tiled=True
        ),
    )
    row_acts = recv_acts.reshape(slot_total, -1)
    row_cot = recv_cot.reshape(slot_total, -1)
    half_acts = row_acts.shape[1] // 2
    row_gate, row_up, row_sigmoid, row_active, hidden_rows = activations(
        row_acts[:, :half_acts], row_acts[:, half_acts:]
    )
    row_dhidden = jnp.dot(row_cot, down_full, preferred_element_type=jnp.float32)
    placed = gate_grads(row_dhidden, row_gate, row_up, row_sigmoid, row_active)
    down_grad = lax.psum_scatter(
        lax.dot_general(
            row_cot, hidden_rows, (((0,), (0,)), ((), ())), preferred_element_type=jnp.float32
        ),
        "dp",
        scatter_dimension=0,
        tiled=True,
    )
    half_width = placed.shape[1] // 2
    return (layer_output, placed[:, :half_width], placed[:, half_width:], down_grad)


def solution(mesh):
    placed = (P("dp", None), P(None, "dp", "mp"), P("dp", "mp"), P("dp", None), P("dp"))
    return jax.shard_map(
        body,
        mesh=mesh,
        in_specs=placed,
        out_specs=(P("dp", "mp"), P("dp", "mp"), P("dp", "mp"), P("dp", "mp")),
        check_vma=False,
    )
```

profile of v0, /device:TPU:1, one launch (start us, length us, event | category | flops | bytes accessed | tf_op | source)
XLA Modules:
  0.0 597.9 jit_solution(14198727453665252784)
XLA Ops:
  7.2 0.0 copy-start
  7.2 0.0 all-gather.3.cloned.1.call-start
  7.2 0.7 all-gather.3.cloned.1.call-update
  7.9 0.8 copy.9
  8.7 0.2 fusion.32
  9.0 0.9 fusion.34
  9.9 0.7 broadcast_compare_fusion
  10.6 0.7 compare_select_fusion
  11.2 2.4 scatter_custom_fusion
  13.7 1.0 reshape.38
  14.7 20.4 %all-to-all-start = ((bf16[128,2,1024]{2,1,0:T(2,128)(2,1)}), bf16[128,2,1024]{2,1,0:T(2,128)(2,1)S(1)}, u32[]{:S(2)}, u32[]{:S(2)}) async-start(bf16[128,2,1024]{2,1,0:T(2,128)(2,1)} %reshape.38), calls=%async_computation.1 | async-start | bytes 1048576 | tf_op jit(solution)/shard_map/all_to_all | solution.py:67
  35.1 0.0 all-gather.5.cloned.1.call-start
  35.1 0.7 all-gather.5.cloned.1.call-update
  35.8 128.7 %all-gather.3.cloned.1.call-done = bf16[2,2048,768]{2,1,0:T(8,128)(2,1)} async-done(((bf16[2,16,768]{2,1,0:T(8,128)(2,1)}), bf16[2,2048,768]{2,1,0:T(8,128)(2,1)}) %all-gather.3.cloned.1.call-update) | async-done | bytes 6291472 | tf_op jit(solution)/shard_map/all_gather | solution.py:26
  164.6 0.0 copy-done
  164.6 0.0 copy-start.3
  164.6 3.0 fusion.2
  167.6 0.7 copy-done.3
  168.3 0.0 copy-start.2
  168.3 1.8 fusion.3
  170.1 0.0 copy-done.2
  170.1 2.5 scatter_custom_fusion.1
  172.5 0.1 slice.36
  172.6 1.2 reshape.40
  173.8 0.0 all-to-all-done
  173.8 9.7 %all-to-all-start.1 = ((bf16[128,2,1536]{2,1,0:T(2,128)(2,1)}), bf16[128,2,1536]{2,1,0:T(2,128)(2,1)S(1)}, u32[]{:S(2)}, u32[]{:S(2)}) async-start(bf16[128,2,1536]{2,1,0:T(2,128)(2,1)} %reshape.40), calls=%async_computation.2 | async-start | bytes 1572864 | tf_op jit(solution)/shard_map/all_to_all | solution.py:64
  183.5 0.0 reduce-scatter.3.cloned.1.call-start
  183.5 122.7 %all-gather.5.cloned.1.call-done = bf16[1024,768]{1,0:T(8,128)(2,1)} async-done(((bf16[8,768]{1,0:T(8,128)(2,1)}), bf16[1024,768]{1,0:T(8,128)(2,1)}) %all-gather.5.cloned.1.call-update) | async-done | bytes 1572880 | tf_op jit(solution)/shard_map/all_gather | solution.py:27
  306.2 3.1 convolution_convert_fusion
  309.3 0.0 reduce-scatter.3.cloned.1.call-update
  309.3 0.0 reduce-scatter.5.cloned.1.call-start
  309.4 1.0 reshape.39
  310.4 0.0 all-to-all-done.1
  310.4 0.3 reshape.41
  310.7 0.0 copy-start.1
  310.7 3.5 fusion.26
  314.1 0.0 reduce-scatter.5.cloned.1.call-update
  314.2 0.0 copy-done.1
  314.2 3.0 multiply_convert_fusion
  317.2 15.6 %reduce-scatter.3.cloned.1.call-done = bf16[256,256]{1,0:T(8,128)(2,1)} async-done(((bf16[256,1024]{1,0:T(8,128)(2,1)}), bf16[256,256]{1,0:T(8,128)(2,1)}) %reduce-scatter.3.cloned.1.call-update) | async-done | bytes 131088 | tf_op jit(solution)/shard_map/reduce_scatter | solution.py:37
  332.8 258.5 %reduce-scatter.5.cloned.1.call-done = f32[8,768]{1,0:T(8,128)} async-done(((f32[1024,768]{1,0:T(8,128)}), f32[8,768]{1,0:T(8,128)}) %reduce-scatter.5.cloned.1.call-update) | async-done | bytes 24592 | tf_op jit(solution)/shard_map/reduce_scatter | solution.py:79
  (7 shorter events, 0.1 us)
Async XLA Ops:
  7.2 157.4 %copy-start = (bf16[256,2048]{1,0:T(8,128)(2,1)S(1)}, bf16[256,2048]{1,0:T(8,128)(2,1)}, u32[]{:S(2)}) copy-start(bf16[256,2048]{1,0:T(8,128)(2,1)} %param.5) | copy-start | bytes 3145732
  7.2 157.4 %all-gather.3.cloned.1.call-start = ((), (), s32[]{:S(2)}) async-start(), calls=%async_computation.4 | async-start | bytes 6340608 | tf_op jit(solution)/shard_map/all_gather | solution.py:26
  14.7 159.1 %all-to-all-start = ((bf16[128,2,1024]{2,1,0:T(2,128)(2,1)}), bf16[128,2,1024]{2,1,0:T(2,128)(2,1)S(1)}, u32[]{:S(2)}, u32[]{:S(2)}) async-start(bf16[128,2,1024]{2,1,0:T(2,128)(2,1)} %reshape.38), calls=%async_computation.1 | async-start | bytes 1048576 | tf_op jit(solution)/shard_map/all_to_all | solution.py:67
  35.1 271.1 %all-gather.5.cloned.1.call-start = ((), (), s32[]{:S(2)}) async-start(), calls=%async_computation.5 | async-start | bytes 1585152 | tf_op jit(solution)/shard_map/all_gather | solution.py:27
  164.6 3.7 copy-start.3
  168.3 1.8 copy-start.2
  173.8 136.6 %all-to-all-start.1 = ((bf16[128,2,1536]{2,1,0:T(2,128)(2,1)}), bf16[128,2,1536]{2,1,0:T(2,128)(2,1)S(1)}, u32[]{:S(2)}, u32[]{:S(2)}) async-start(bf16[128,2,1536]{2,1,0:T(2,128)(2,1)} %reshape.40), calls=%async_computation.2 | async-start | bytes 1572864 | tf_op jit(solution)/shard_map/all_to_all | solution.py:64
  183.5 149.3 %reduce-scatter.3.cloned.1.call-start = ((), (), s32[]{:S(2)}) async-start(), calls=%async_computation.6 | async-start | bytes 655360 | tf_op jit(solution)/shard_map/reduce_scatter | solution.py:37
  309.3 282.0 %reduce-scatter.5.cloned.1.call-start = ((), (), s32[]{:S(2)}) async-start(), calls=%async_computation.7 | async-start | bytes 3170304 | tf_op jit(solution)/shard_map/reduce_scatter | solution.py:79
  310.7 3.5 copy-start.1
Sparse Core Ops, SparseCore 0:
  11.2 153.3 all-gather.2
  167.6 138.5 all-gather.4
  309.6 23.1 reduce-scatter.2
  337.9 253.4 reduce-scatter.4
where the time goes:
time: 609 us; the launch traced here: 598 us
  waiting for transfers between devices  527 us (87%)
  starting transfers between devices  30.2 us (5%)
  matrix products  14.3 us (2%)
  between operations  13.9 us (2%)
  other arithmetic  7.31 us (1%)
    reduce_scatter x1, waiting for transfers between devices, body(): lax.psum_scatter(lax.dot_general(row_cot, hidden_rows, (((0,), (0,)), (()...  259 us
    all_gather x1, waiting for transfers between devices, body(): lax.all_gather(inner_weights, 'dp', axis=1, tiled=True)  129 us
    all_gather x1, waiting for transfers between devices, body(): lax.all_gather(down_weight, 'dp', axis=0, tiled=True)  123 us
    all_to_all x1, starting transfers between devices, body(): lax.all_to_all(send_cot.reshape(shards, capacity, -1), 'dp', split_axis=0...  20.4 us
    reduce_scatter x1, waiting for transfers between devices, body(): lax.psum_scatter(partial_value.astype(jnp.bfloat16), 'mp', scatter_dimens...  15.6 us
  transfers between devices with their start and end apart: 6, of which 4 were waited for; matrix products, arithmetic and copies ran while one was open for 4% of the time, Pallas kernels for 0%

commit v1 on v0

v1 whole, which is shorter than its diff:
```python
import jax
import jax.numpy as jnp
from jax import lax
from jax.experimental import pallas as pl
from jax.experimental.pallas import tpu as pltpu
from jax.sharding import PartitionSpec as P

BF = jnp.bfloat16
F32 = jnp.float32
MESH = pl.DeviceIdType.MESH

NZ, NX, NY = 16, 4, 4
NQ = NX * 2
TOK = 256
D = 2048
HID = 768
DW = 1024
SQ = D // NY
CQ = DW // NY
WQ = SQ + CQ
TILE = 256
LAGX = 2
LAGS = 4


def z_offset(i):
    return -((i + 1) // 2) if i % 2 else i // 2


def goes_right(i):
    return i == 0 or (i % 2 == 1 and i < NZ - 1)


def kernel(
    routes_ref, states_ref, inner_ref, down_ref, cot_ref,
    layer_ref, gates_ref, linear_ref, dgrad_ref,
    w, dn, dsib, s_buf, r1, t_buf, r2, rows, hidden, ct, ctp32, ctp,
    p_send, p_recv, p_own, x_send, x_recv, x_own, z_send, z_recv, l_send, l_recv,
    sib0_s, sib0_r, zs, zr, xls, xlr, xrs, xrr, x2s, x2r, sbs, sbr,
    a1s, a1r, a2s, a2r, a3s, a3r, p0s, p0r, p1s, p1r, p2s, p2r, ls, lr,
):
    d, y = lax.axis_index("dp"), lax.axis_index("mp")
    c, x, z = lax.rem(d, 2), lax.rem(d // 2, NX), d // NQ
    q = lax.rem(d, NQ)

    def dev(zz, xx, cc):
        return ((zz * NX + xx) * 2 + cc, y)

    def plus(a, k, n):
        return lax.rem(a + (k + n), n)

    def remote(src, dst, send, recv, to):
        return pltpu.make_async_remote_copy(
            src_ref=src, dst_ref=dst, send_sem=send, recv_sem=recv, device_id=to, device_id_type=MESH
        )

    right, left = dev(z, plus(x, 1, NX), c), dev(z, plus(x, -1, NX), c)
    up, down = dev(plus(z, 1, NZ), x, c), dev(plus(z, -1, NZ), x, c)
    sibling = dev(z, x, 1 - c)

    barrier = pltpu.get_barrier_semaphore()
    for k in range(1, NZ):
        pl.semaphore_signal(barrier, inc=1, device_id=dev(plus(z, k, NZ), x, c), device_id_type=MESH)
    for k in range(1, NQ):
        qq = plus(q, k, NQ)
        pl.semaphore_signal(barrier, inc=1, device_id=(z * NQ + qq, y), device_id_type=MESH)
    for k in range(1, NY):
        pl.semaphore_signal(barrier, inc=1, device_id=(d, plus(y, k, NY)), device_id_type=MESH)
    pl.semaphore_wait(barrier, NZ + NQ + NY - 3)

    def chunk(zz, xx, lane):
        at = zz * NX + xx
        return (
            w.at[lane, pl.ds(pl.multiple_of(at * 32, 32), 32), :],
            dn.at[pl.ds(pl.multiple_of(at * 16, 16), 16), pl.ds(pl.multiple_of(lane * 384, 128), 384)],
        )

    def group(zz, lane):
        return (
            w.at[lane, pl.ds(pl.multiple_of(zz * 128, 128), 128), :],
            dn.at[pl.ds(pl.multiple_of(zz * 64, 64), 64), pl.ds(pl.multiple_of(lane * 384, 128), 384)],
        )

    def move(refs, send, recv, i, to):
        return [remote(r, r, send.at[j, i], recv.at[j, i], to) for j, r in enumerate(refs)]

    sends = []

    def start(copies):
        for one in copies:
            one.start()
        sends.extend(copies)

    def arrive(copies):
        for one in copies:
            one.wait_recv()

    own_row = pl.multiple_of((z * NX + x) * 32 + c * 16, 16)
    sib_copies = [
        remote(
            inner_ref.at[1 - c], w.at[1 - c, pl.ds(own_row, 16), :], sib0_s.at[0], sib0_r.at[0], sibling
        ),
        remote(down_ref, dsib, sib0_s.at[1], sib0_r.at[1], sibling),
    ]
    start(sib_copies)
    w[c, pl.ds(own_row, 16), :] = inner_ref[c]

    r_row = jnp.broadcast_to(routes_ref[...].astype(F32), (TOK, TOK))
    r_col = r_row.T
    sub = lax.broadcasted_iota(jnp.int32, (TOK, TOK), 0)
    lane_i = lax.broadcasted_iota(jnp.int32, (TOK, TOK), 1)
    before = jnp.where((r_row == r_col) & (sub < lane_i), 1.0, 0.0)
    count = jnp.sum(before, axis=0, keepdims=True)
    slot = jnp.where(r_row >= 0, r_row * 2.0 + count, -1.0)
    pick = jnp.where(slot == sub.astype(F32), 1.0, 0.0).astype(BF)
    part = jnp.dot(
        pick, states_ref[:, pl.ds(pl.multiple_of(y * SQ, SQ), SQ)], preferred_element_type=F32
    ).astype(BF)
    s_buf[:, :, :SQ] = part.reshape(NZ, 16, SQ)
    part = jnp.dot(
        pick, cot_ref[:, pl.ds(pl.multiple_of(y * CQ, CQ), CQ)], preferred_element_type=F32
    ).astype(BF)
    s_buf[:, :, SQ:] = part.reshape(NZ, 16, CQ)
    r1[pl.ds(z, 1)] = s_buf[pl.ds(z, 1)]

    theirs = [
        remote(
            inner_ref.at[c],
            w.at[c, pl.ds(pl.multiple_of((z * NX + x) * 32 + (1 - c) * 16, 16), 16), :],
            sib0_s.at[0],
            sib0_r.at[0],
            sibling,
        ),
        sib_copies[1],
    ]
    arrive(theirs)
    mine32, sib32 = down_ref[...].astype(F32), dsib[...].astype(F32)
    first, second = jnp.where(c == 0, mine32, sib32), jnp.where(c == 0, sib32, mine32)
    both = jnp.concatenate([first, second], axis=0)
    both = jnp.where(c == 0, both[:, :384], both[:, 384:]).astype(BF)
    dn[
        pl.ds(pl.multiple_of((z * NX + x) * 16, 16), 16), pl.ds(pl.multiple_of(c * 384, 128), 384)
    ] = both

    def send_z(i):
        own = chunk(plus(z, z_offset(i), NZ), x, c)
        if i == 0:
            start(move(own, zs, zr, 1, up))
            start(move(own, zs, zr, 2, down))
        elif i % 2 and i + 2 < NZ:
            start(move(own, zs, zr, i + 2, up))
        elif i % 2 == 0 and i + 2 < NZ - 1:
            start(move(own, zs, zr, i + 2, down))

    def send_x(i):
        own = chunk(plus(z, z_offset(i), NZ), x, c)
        start(move(own, xls, xlr, i, right))
        start(move(own, xrs, xrr, i, left))

    def pass_x(i):
        zz = plus(z, z_offset(i), NZ)
        from_left, from_right = chunk(zz, plus(x, -1, NX), c), chunk(zz, plus(x, 1, NX), c)
        arrive(move(from_left, xls, xlr, i, right))
        arrive(move(from_right, xrs, xrr, i, left))
        if goes_right(i):
            start(move(from_left, x2s, x2r, i, right))
        else:
            start(move(from_right, x2s, x2r, i, left))

    def to_sibling(i):
        zz = plus(z, z_offset(i), NZ)
        arrive(move(chunk(zz, plus(x, 2, NX), c), x2s, x2r, i, right))
        start(move(group(zz, c), sbs, sbr, i, sibling))

    def rows_z(k):
        to = plus(z, k, NZ)
        start([remote(s_buf.at[to], r1.at[z], a1s.at[k], a1r.at[k], dev(to, x, c))])

    def permuted(values, out_first):
        low = sub % out_first
        src = (low // 2) * (TOK // (out_first // 2)) + (sub // out_first) * 2 + sub % 2
        matrix = jnp.where(src == lane_i, 1.0, 0.0).astype(BF)
        return jnp.dot(matrix, values, preferred_element_type=F32).astype(BF)

    def rows_q():
        for k in range(1, NZ):
            at = plus(z, -k, NZ)
            arrive([remote(s_buf.at[at], r1.at[at], a1s.at[k], a1r.at[k], dev(at, x, c))])
        t_buf[...] = permuted(r1[...].reshape(TOK, WQ), 32).reshape(NQ, 32, WQ)
        r2[pl.ds(q, 1)] = t_buf[pl.ds(q, 1)]
        for k in range(1, NQ):
            to = plus(q, k, NQ)
            start([remote(t_buf.at[to], r2.at[q], a2s.at[k], a2r.at[k], (z * NQ + to, y))])

    def rows_y():
        for k in range(1, NQ):
            at = plus(q, -k, NQ)
            arrive([remote(t_buf.at[at], r2.at[at], a2s.at[k], a2r.at[k], (z * NQ + at, y))])
        rows[pl.ds(y, 1)] = permuted(r2[...].reshape(TOK, WQ), 16).reshape(1, TOK, WQ)
        for k in range(1, NY):
            start([remote(rows.at[y], rows.at[y], a3s.at[k], a3r.at[k], (d, plus(y, k, NY)))])

    def rows_done():
        for k in range(1, NY):
            at = plus(y, -k, NY)
            arrive([remote(rows.at[at], rows.at[at], a3s.at[k], a3r.at[k], (d, at))])

    def transpose_cot():
        keep = r_col >= 0
        for j in range(DW // TILE):
            cols = slice(j * TILE, (j + 1) * TILE)
            ct[cols, :] = jnp.where(keep, cot_ref[:, cols].astype(F32), 0.0).T

        def one(n, carry):
            zz, xx, cc = n // NQ, (n // 2) % NX, n % 2
            to = (cc * NX + xx) * NZ + zz
            ctp32[pl.ds(pl.multiple_of(to * 8, 8), 8), :] = ct[pl.ds(pl.multiple_of(n * 8, 8), 8), :]
            return carry

        lax.fori_loop(0, NZ * NQ, one, 0)
        ctp[...] = ctp32[...].astype(BF)

    for i in range(NZ + LAGS):
        if i < NZ:
            if i > 0:
                arrive(move(chunk(plus(z, z_offset(i), NZ), x, c), zs, zr, i, up))
            send_z(i)
            send_x(i)
        if i < 8:
            for k in (2 * i + 1, 2 * i + 2):
                if k < NZ:
                    rows_z(k)
        if 0 <= i - LAGX < NZ:
            pass_x(i - LAGX)
        if 0 <= i - LAGS < NZ:
            to_sibling(i - LAGS)
        if i == 3:
            transpose_cot()
        if i == 10:
            rows_q()
        if i == 14:
            rows_y()
    for i in range(NZ):
        arrive(move(group(plus(z, z_offset(i), NZ), 1 - c), sbs, sbr, i, sibling))

    def preacts(gate_f32, up_f32):
        gate = gate_f32.astype(BF).astype(F32)
        up_value = up_f32.astype(BF).astype(F32)
        sig = jax.nn.sigmoid(gate)
        return gate, up_value, sig, gate * sig

    def columns(t):
        return pl.ds(pl.multiple_of(t * TILE, TILE), TILE)

    def forward(t, carry):
        cols = columns(t)
        _, up_value, _, active = preacts(
            jnp.dot(states_ref[...], w[0, :, cols], preferred_element_type=F32),
            jnp.dot(states_ref[...], w[1, :, cols], preferred_element_type=F32),
        )
        hidden[:, cols] = (active * up_value).astype(BF)
        return carry

    lax.fori_loop(0, HID // TILE, forward, 0)

    half = DW // 2

    def other_half(m, carry):
        at = pl.multiple_of((1 - c) * half + m * TILE, TILE)
        p_send[pl.ds(pl.multiple_of(m * TILE, TILE), TILE), :] = jnp.dot(
            ctp[pl.ds(at, TILE), :], hidden[...], preferred_element_type=F32
        ).astype(BF)
        return carry

    lax.fori_loop(0, half // TILE, other_half, 0)
    to_other = [remote(p_send, p_recv, p0s.at[0], p0r.at[0], sibling)]
    start(to_other)

    def layer_part(yy):
        return lax.dot_general(
            hidden[...],
            dn[pl.ds(pl.multiple_of(yy * TILE, TILE), TILE), :],
            (((1,), (1,)), ((), ())),
            preferred_element_type=F32,
        ).astype(BF)

    layer_copies = []
    for k in range(1, NY):
        to = plus(y, k, NY)
        l_send[k] = layer_part(to)
        layer_copies.append(remote(l_send.at[k], l_recv.at[k], ls.at[k], lr.at[k], (d, to)))
        start(layer_copies[-1:])
    l_send[0] = layer_part(y)

    def own_half(m, carry):
        at = pl.multiple_of(c * half + m * TILE, TILE)
        p_own[pl.ds(pl.multiple_of(m * TILE, TILE), TILE), :] = jnp.dot(
            ctp[pl.ds(at, TILE), :], hidden[...], preferred_element_type=F32
        )
        return carry

    lax.fori_loop(0, half // TILE, own_half, 0)
    arrive(to_other)
    x_copies = []
    for k in range(1, NX):
        to = plus(x, k, NX)
        at = pl.ds(pl.multiple_of(to * 128, 128), 128)
        x_send[k] = (p_own[at, :] + p_recv[at, :].astype(F32)).astype(BF)
        x_copies.append(remote(x_send.at[k], x_recv.at[k], p1s.at[k], p1r.at[k], dev(z, to, c)))
        start(x_copies[-1:])
    at = pl.ds(pl.multiple_of(x * 128, 128), 128)
    x_own[...] = p_own[at, :] + p_recv[at, :].astype(F32)

    rows_done()

    def backward(t, carry):
        cols = columns(t)
        gate = jnp.zeros((TOK, TILE), F32)
        up_value = jnp.zeros((TOK, TILE), F32)
        d_hidden = jnp.zeros((TOK, TILE), F32)
        for yy in range(NY):
            gate += jnp.dot(
                rows[yy, :, :SQ], w[0, yy * SQ : (yy + 1) * SQ, cols], preferred_element_type=F32
            )
            up_value += jnp.dot(
                rows[yy, :, :SQ], w[1, yy * SQ : (yy + 1) * SQ, cols], preferred_element_type=F32
            )
            d_hidden += jnp.dot(
                rows[yy, :, SQ:], dn[yy * CQ : (yy + 1) * CQ, cols], preferred_element_type=F32
            )
        gate, up_value, sig, active = preacts(gate, up_value)
        gates_ref[:, cols] = (d_hidden * up_value * (sig * (1.0 + gate * (1.0 - sig)))).astype(BF)
        linear_ref[:, cols] = (d_hidden * active).astype(BF)
        return carry

    lax.fori_loop(0, 1, backward, 0)

    arrive(x_copies)
    x_own[...] = (
        x_own[...] + x_recv[1].astype(F32) + x_recv[2].astype(F32) + x_recv[3].astype(F32)
    )
    z_copies = []
    for k in range(1, NZ):
        to = plus(z, k, NZ)
        piece = x_own[pl.ds(pl.multiple_of(to * 8, 8), 8), :]
        z_send[k] = jnp.concatenate([piece[:, :384], piece[:, 384:]], axis=0).astype(BF)
        z_copies.append(remote(z_send.at[k], z_recv.at[k], p2s.at[k], p2r.at[k], dev(to, x, c)))
        start(z_copies[-1:])

    lax.fori_loop(1, HID // TILE, backward, 0)

    arrive(layer_copies)
    layer_ref[...] = (
        l_send[0].astype(F32)
        + l_recv[1].astype(F32)
        + l_recv[2].astype(F32)
        + l_recv[3].astype(F32)
    ).astype(BF)

    arrive(z_copies)
    total = z_recv[1].astype(F32)
    for k in range(2, NZ):
        total += z_recv[k].astype(F32)
    mine = x_own[pl.ds(pl.multiple_of(z * 8, 8), 8), :]
    dgrad_ref[:, :384] = mine[:, :384] + total[:8]
    dgrad_ref[:, 384:] = mine[:, 384:] + total[8:]

    for one in sends:
        one.wait_send()


def body(states, inner_weights, down_weight, cotangent, routes):
    dma = lambda *shape: pltpu.SemaphoreType.DMA(shape)
    vm = lambda shape, kind=BF: pltpu.VMEM(shape, kind)
    return pl.pallas_call(
        kernel,
        out_shape=(
            jax.ShapeDtypeStruct((TOK, DW // NY), BF),
            jax.ShapeDtypeStruct((TOK, HID), BF),
            jax.ShapeDtypeStruct((TOK, HID), BF),
            jax.ShapeDtypeStruct((DW // 128, HID), F32),
        ),
        in_specs=[pl.BlockSpec(memory_space=pltpu.VMEM)] * 5,
        out_specs=tuple(pl.BlockSpec(memory_space=pltpu.VMEM) for _ in range(4)),
        scratch_shapes=[
            vm((2, D, HID)),
            vm((DW, HID)),
            vm((8, HID)),
            vm((NZ, 16, WQ)),
            vm((NZ, 16, WQ)),
            vm((NQ, 32, WQ)),
            vm((NQ, 32, WQ)),
            vm((NY, TOK, WQ)),
            vm((TOK, HID)),
            vm((DW, TOK), F32),
            vm((DW, TOK), F32),
            vm((DW, TOK)),
            vm((DW // 2, HID)),
            vm((DW // 2, HID)),
            vm((DW // 2, HID), F32),
            vm((NX, 128, HID)),
            vm((NX, 128, HID)),
            vm((128, HID), F32),
            vm((NZ, 16, HID // 2)),
            vm((NZ, 16, HID // 2)),
            vm((NY, TOK, DW // NY)),
            vm((NY, TOK, DW // NY)),
            dma(2),
            dma(2),
        ]
        + [dma(2, NZ)] * 10
        + [dma(NZ), dma(NZ), dma(NQ), dma(NQ), dma(NY), dma(NY)]
        + [dma(1), dma(1), dma(NX), dma(NX), dma(NZ), dma(NZ), dma(NY), dma(NY)],
        compiler_params=pltpu.CompilerParams(
            collective_id=0, has_side_effects=True, vmem_limit_bytes=48 * 1024 * 1024
        ),
    )(routes.reshape(1, TOK), states, inner_weights, down_weight, cotangent)


def solution(mesh):
    return jax.shard_map(
        body,
        mesh=mesh,
        in_specs=(P("dp", None), P(None, "dp", "mp"), P("dp", "mp"), P("dp", None), P("dp")),
        out_specs=(P("dp", "mp"), P("dp", "mp"), P("dp", "mp"), P("dp", "mp")),
        check_vma=False,
    )
```

time: 609 us -> 112 us (0.18); the launches traced: 598 us -> 111 us
  waiting for transfers between devices: 527 us -> 0 us
  Pallas kernels: 0 us -> 103 us
  starting transfers between devices: 30.2 us -> 0 us
  matrix products: 14.3 us -> 0 us
  between operations: 13.9 us -> 0.65 us
  other arithmetic: 7.31 us -> 0 us
    reduce_scatter x2 -> x0, waiting for transfers between devices: 274 us -> none  [the longest x1 259 us: body(): lax.psum_scatter(lax.dot_general(row_cot, hidden_rows, (((0,), (0,)), (()...]
    all_gather x2 -> x0, waiting for transfers between devices: 251 us -> none  [the longest x1 129 us: body(): lax.all_gather(inner_weights, 'dp', axis=1, tiled=True)]
    pallas_call x0 -> x1, Pallas kernels: none -> 103 us  [body(): pl.pallas_call(kernel, out_shape=(jax.ShapeDtypeStruct((TOK, DW // NY), B...]
    all_to_all x2 -> x0, starting transfers between devices: 30.1 us -> none  [the longest x1 20.4 us: body(): lax.all_to_all(send_cot.reshape(shards, capacity, -1), 'dp', split_axis=0...]
    dot_general x5 -> x0, matrix products: 14.3 us -> none  [the longest x1 3.48 us: body(): lax.dot_general(row_cot, hidden_rows, (((0,), (0,)), ((), ())), preferred...]
    unnamed x9 -> x14, local copies, waits for them, and re-layouts: 0.74 us -> 7.2 us
  transfers between devices with their start and end apart: 6 -> 0, of which waited for: 4 -> 0; matrix products, arithmetic and copies ran while one was open for 4% -> 0% of each run, Pallas kernels for 0% -> 0%
where the time goes in v1:
time: 112 us; the launch traced here: 111 us
  Pallas kernels  103 us (92%)
  local copies, waits for them, and re-layouts  7.2 us (6%)
    pallas_call x1, Pallas kernels, body(): pl.pallas_call(kernel, out_shape=(jax.ShapeDtypeStruct((TOK, DW // NY), B...  103 us
    unnamed x14, local copies, waits for them, and re-layouts  7.2 us

profile of v1, /device:TPU:1, one launch (start us, length us, event | category | flops | bytes accessed | tf_op | source)
XLA Modules:
  0.0 111.3 jit_solution(5726788330321488570)
XLA Ops:
  0.6 0.0 copy-start.4
  0.6 0.7 copy-done.4
  1.3 0.0 copy-start
  1.3 1.2 %copy-done = bf16[256,2048]{1,0:T(8,128)(2,1)S(1)} copy-done((bf16[256,2048]{1,0:T(8,128)(2,1)S(1)}, bf16[256,2048]{1,0:T(8,128)(2,1)}, u32[]{:S(2)}) %copy-start) | copy-done | bytes 1048600
  2.5 0.0 copy-start.1
  2.5 1.0 copy-done.1
  3.6 0.0 copy-start.2
  3.6 0.8 copy-done.2
  4.4 0.0 copy-start.3
  4.4 0.7 copy-done.3
  5.1 103.4 %shard_map.84 = (bf16[256,256]{1,0:T(8,128)(2,1)S(1)}, bf16[256,768]{1,0:T(8,128)(2,1)S(1)}, bf16[256,768]{1,0:T(8,128)(2,1)S(1)}, f32[8,768]{1,0:T(8,128)S(1)}) custom-call(s32[1,256]{1,0:T(1,128)S(1)} %bitcast.1, bf16[256,2048]{1,0:T(8,128)(2,1)S(1)} %copy-done, bf16[2,16,768]{2,1,0:T(8,128)(2,1)S(1)} %copy-done.2, bf16[8,768]{1,0:T(8,128)(2,1)S(1)} %copy-done.3, ...), custom_call_target="tpu_custom_call" | custom-call | tf_op jit(solution)/shard_map/pallas_call | solution.py:375
  108.5 0.7 copy.13
  109.2 0.7 copy.14
  109.9 0.7 copy.15
  110.7 0.6 copy.16
Async XLA Ops:
  0.6 0.7 copy-start.4
  1.3 1.2 %copy-start = (bf16[256,2048]{1,0:T(8,128)(2,1)S(1)}, bf16[256,2048]{1,0:T(8,128)(2,1)}, u32[]{:S(2)}) copy-start(bf16[256,2048]{1,0:T(8,128)(2,1)} %states_ref.1) | copy-start | bytes 3145732
  2.5 1.0 copy-start.1
  3.6 0.8 copy-start.2
  4.4 0.7 copy-start.3

commit v2 on v1

--- a/solution.py
+++ b/solution.py
@@ -17,26 +17,35 @@
 DW = 1024
 SQ = D // NY
 CQ = DW // NY
-WQ = SQ + CQ
 TILE = 256
+
+ORDER = (0, -1, 1, -2, 2, -3, 3, -4, 4, -5, 5, -6, 6, -7, 7, 8)
+NEXT = {0: ((1, -1), (-1, 1)), -7: ((1, 8),)}
+for _k in range(1, 7):
+    NEXT[-_k] = ((1, -_k - 1),)
+    NEXT[_k] = ((-1, _k + 1),)
+PIECES = 3
+AT_Q, AT_Y = (10, 15, 20), (15, 20, 21)
+PER_STEP = 3
+FAR = [k for j in range(1, NZ // 2) for k in (j, NZ - j)] + [NZ // 2]
+TURN = 4
 LAGX = 2
 LAGS = 4
-
-
-def z_offset(i):
-    return -((i + 1) // 2) if i % 2 else i // 2
+LAGD = 3
+LAST = NZ + 4
 
 
 def goes_right(i):
-    return i == 0 or (i % 2 == 1 and i < NZ - 1)
+    return ORDER[i] <= 0
 
 
 def kernel(
-    routes_ref, states_ref, inner_ref, down_ref, cot_ref,
+    routes_in, states_in, inner_in, down_in, cot_in,
     layer_ref, gates_ref, linear_ref, dgrad_ref,
+    routes_ref, states_ref, inner_ref, down_ref, cot_ref, in_sem,
     w, dn, dsib, s_buf, r1, t_buf, r2, rows, hidden, ct, ctp32, ctp,
     p_send, p_recv, p_own, x_send, x_recv, x_own, z_send, z_recv, l_send, l_recv,
-    sib0_s, sib0_r, zs, zr, xls, xlr, xrs, xrr, x2s, x2r, sbs, sbr,
+    sib0_s, sib0_r, zs, zr, xls, xlr, xrs, xrr, x2s, x2r, sbs, sbr, dxs, dxr, dzs, dzr, dss, dsr,
     a1s, a1r, a2s, a2r, a3s, a3r, p0s, p0r, p1s, p1r, p2s, p2r, ls, lr,
 ):
     d, y = lax.axis_index("dp"), lax.axis_index("mp")
@@ -55,8 +64,18 @@
         )
 
     right, left = dev(z, plus(x, 1, NX), c), dev(z, plus(x, -1, NX), c)
-    up, down = dev(plus(z, 1, NZ), x, c), dev(plus(z, -1, NZ), x, c)
     sibling = dev(z, x, 1 - c)
+
+    pairs = (
+        (inner_in, inner_ref),
+        (down_in, down_ref),
+        (routes_in, routes_ref),
+        (states_in, states_ref),
+        (cot_in, cot_ref),
+    )
+    loads = [pltpu.make_async_copy(a, b, in_sem.at[i]) for i, (a, b) in enumerate(pairs)]
+    for one in loads:
+        one.start()
 
     barrier = pltpu.get_barrier_semaphore()
     for k in range(1, NZ):
@@ -69,20 +88,22 @@
     pl.semaphore_wait(barrier, NZ + NQ + NY - 3)
 
     def chunk(zz, xx, lane):
-        at = zz * NX + xx
-        return (
-            w.at[lane, pl.ds(pl.multiple_of(at * 32, 32), 32), :],
-            dn.at[pl.ds(pl.multiple_of(at * 16, 16), 16), pl.ds(pl.multiple_of(lane * 384, 128), 384)],
-        )
+        return w.at[lane, pl.ds(pl.multiple_of((zz * NX + xx) * 32, 32), 32), :]
 
     def group(zz, lane):
-        return (
-            w.at[lane, pl.ds(pl.multiple_of(zz * 128, 128), 128), :],
-            dn.at[pl.ds(pl.multiple_of(zz * 64, 64), 64), pl.ds(pl.multiple_of(lane * 384, 128), 384)],
-        )
-
-    def move(refs, send, recv, i, to):
-        return [remote(r, r, send.at[j, i], recv.at[j, i], to) for j, r in enumerate(refs)]
+        return w.at[lane, pl.ds(pl.multiple_of(zz * 128, 128), 128), :]
+
+    def lanes(lane):
+        return pl.ds(pl.multiple_of(lane * 384, 128), 384)
+
+    def down_chunk(xx):
+        return dn.at[pl.ds(pl.multiple_of((z * NX + xx) * 16, 16), 16), lanes(c)]
+
+    def down_group(zz, lane):
+        return dn.at[pl.ds(pl.multiple_of(zz * 64, 64), 64), lanes(lane)]
+
+    def move(ref, send, recv, i, to):
+        return [remote(ref, ref, send.at[i], recv.at[i], to)]
 
     sends = []
 
@@ -95,6 +116,8 @@
         for one in copies:
             one.wait_recv()
 
+    loads[0].wait()
+    loads[1].wait()
     own_row = pl.multiple_of((z * NX + x) * 32 + c * 16, 16)
     sib_copies = [
         remote(
@@ -105,6 +128,8 @@
     start(sib_copies)
     w[c, pl.ds(own_row, 16), :] = inner_ref[c]
 
+    for one in loads[2:]:
+        one.wait()
     r_row = jnp.broadcast_to(routes_ref[...].astype(F32), (TOK, TOK))
     r_col = r_row.T
     sub = lax.broadcasted_iota(jnp.int32, (TOK, TOK), 0)
@@ -113,15 +138,14 @@
     count = jnp.sum(before, axis=0, keepdims=True)
     slot = jnp.where(r_row >= 0, r_row * 2.0 + count, -1.0)
     pick = jnp.where(slot == sub.astype(F32), 1.0, 0.0).astype(BF)
-    part = jnp.dot(
-        pick, states_ref[:, pl.ds(pl.multiple_of(y * SQ, SQ), SQ)], preferred_element_type=F32
-    ).astype(BF)
-    s_buf[:, :, :SQ] = part.reshape(NZ, 16, SQ)
-    part = jnp.dot(
-        pick, cot_ref[:, pl.ds(pl.multiple_of(y * CQ, CQ), CQ)], preferred_element_type=F32
-    ).astype(BF)
-    s_buf[:, :, SQ:] = part.reshape(NZ, 16, CQ)
-    r1[pl.ds(z, 1)] = s_buf[pl.ds(z, 1)]
+    for p in range(PIECES):
+        if p < 2:
+            values = states_ref[:, pl.ds(pl.multiple_of(y * SQ + p * TILE, TILE), TILE)]
+        else:
+            values = cot_ref[:, pl.ds(pl.multiple_of(y * CQ, CQ), CQ)]
+        part = jnp.dot(pick, values, preferred_element_type=F32).astype(BF)
+        s_buf[p] = part.reshape(NZ, 16, TILE)
+        r1[p, pl.ds(z, 1)] = s_buf[p, pl.ds(z, 1)]
 
     theirs = [
         remote(
@@ -138,27 +162,19 @@
     first, second = jnp.where(c == 0, mine32, sib32), jnp.where(c == 0, sib32, mine32)
     both = jnp.concatenate([first, second], axis=0)
     both = jnp.where(c == 0, both[:, :384], both[:, 384:]).astype(BF)
-    dn[
-        pl.ds(pl.multiple_of((z * NX + x) * 16, 16), 16), pl.ds(pl.multiple_of(c * 384, 128), 384)
-    ] = both
-
-    def send_z(i):
-        own = chunk(plus(z, z_offset(i), NZ), x, c)
-        if i == 0:
-            start(move(own, zs, zr, 1, up))
-            start(move(own, zs, zr, 2, down))
-        elif i % 2 and i + 2 < NZ:
-            start(move(own, zs, zr, i + 2, up))
-        elif i % 2 == 0 and i + 2 < NZ - 1:
-            start(move(own, zs, zr, i + 2, down))
+    dn[pl.ds(pl.multiple_of((z * NX + x) * 16, 16), 16), lanes(c)] = both
+
+    def send_z(ref, send, recv, i):
+        for step, there in NEXT.get(ORDER[i], ()):
+            start(move(ref, send, recv, ORDER.index(there), dev(plus(z, step, NZ), x, c)))
 
     def send_x(i):
-        own = chunk(plus(z, z_offset(i), NZ), x, c)
+        own = chunk(plus(z, ORDER[i], NZ), x, c)
         start(move(own, xls, xlr, i, right))
         start(move(own, xrs, xrr, i, left))
 
     def pass_x(i):
-        zz = plus(z, z_offset(i), NZ)
+        zz = plus(z, ORDER[i], NZ)
         from_left, from_right = chunk(zz, plus(x, -1, NX), c), chunk(zz, plus(x, 1, NX), c)
         arrive(move(from_left, xls, xlr, i, right))
         arrive(move(from_right, xrs, xrr, i, left))
@@ -168,13 +184,35 @@
             start(move(from_right, x2s, x2r, i, left))
 
     def to_sibling(i):
-        zz = plus(z, z_offset(i), NZ)
+        zz = plus(z, ORDER[i], NZ)
         arrive(move(chunk(zz, plus(x, 2, NX), c), x2s, x2r, i, right))
         start(move(group(zz, c), sbs, sbr, i, sibling))
 
-    def rows_z(k):
-        to = plus(z, k, NZ)
-        start([remote(s_buf.at[to], r1.at[z], a1s.at[k], a1r.at[k], dev(to, x, c))])
+    onward = 1 - 2 * c
+
+    def down_x():
+        start(move(down_chunk(x), dxs, dxr, 0, right))
+        start(move(down_chunk(x), dxs, dxr, 1, left))
+
+    def down_x2():
+        arrive(move(down_chunk(plus(x, -1, NX)), dxs, dxr, 0, right))
+        arrive(move(down_chunk(plus(x, 1, NX)), dxs, dxr, 1, left))
+        start(move(down_chunk(plus(x, -onward, NX)), dxs, dxr, 2, dev(z, plus(x, onward, NX), c)))
+
+    def down_z(i):
+        ref = down_group(plus(z, ORDER[i], NZ), c)
+        if i == 0:
+            arrive(move(down_chunk(plus(x, 2, NX)), dxs, dxr, 2, right))
+        else:
+            arrive(move(ref, dzs, dzr, i, right))
+        send_z(ref, dzs, dzr, i)
+        start(move(ref, dss, dsr, i, sibling))
+
+    def rows_z(i):
+        for n in range(i * PER_STEP, min((i + 1) * PER_STEP, PIECES * (NZ - 1))):
+            p, k = n // (NZ - 1), FAR[n % (NZ - 1)]
+            to = plus(z, k, NZ)
+            start([remote(s_buf.at[p, to], r1.at[p, z], a1s.at[p, k], a1r.at[p, k], dev(to, x, c))])
 
     def permuted(values, out_first):
         low = sub % out_first
@@ -182,28 +220,36 @@
         matrix = jnp.where(src == lane_i, 1.0, 0.0).astype(BF)
         return jnp.dot(matrix, values, preferred_element_type=F32).astype(BF)
 
-    def rows_q():
+    def rows_q(p):
         for k in range(1, NZ):
             at = plus(z, -k, NZ)
-            arrive([remote(s_buf.at[at], r1.at[at], a1s.at[k], a1r.at[k], dev(at, x, c))])
-        t_buf[...] = permuted(r1[...].reshape(TOK, WQ), 32).reshape(NQ, 32, WQ)
-        r2[pl.ds(q, 1)] = t_buf[pl.ds(q, 1)]
+            arrive([remote(s_buf.at[p, at], r1.at[p, at], a1s.at[p, k], a1r.at[p, k], dev(at, x, c))])
+        t_buf[p] = permuted(r1[p].reshape(TOK, TILE), 32).reshape(NQ, 32, TILE)
+        r2[p, pl.ds(q, 1)] = t_buf[p, pl.ds(q, 1)]
         for k in range(1, NQ):
             to = plus(q, k, NQ)
-            start([remote(t_buf.at[to], r2.at[q], a2s.at[k], a2r.at[k], (z * NQ + to, y))])
-
-    def rows_y():
+            start([remote(t_buf.at[p, to], r2.at[p, q], a2s.at[p, k], a2r.at[p, k], (z * NQ + to, y))])
+
+    def rows_y(p):
         for k in range(1, NQ):
             at = plus(q, -k, NQ)
-            arrive([remote(t_buf.at[at], r2.at[at], a2s.at[k], a2r.at[k], (z * NQ + at, y))])
-        rows[pl.ds(y, 1)] = permuted(r2[...].reshape(TOK, WQ), 16).reshape(1, TOK, WQ)
+            arrive([remote(t_buf.at[p, at], r2.at[p, at], a2s.at[p, k], a2r.at[p, k], (z * NQ + at, y))])
+        rows[p, pl.ds(y, 1)] = permuted(r2[p].reshape(TOK, TILE), 16).reshape(1, TOK, TILE)
         for k in range(1, NY):
-            start([remote(rows.at[y], rows.at[y], a3s.at[k], a3r.at[k], (d, plus(y, k, NY)))])
+            mine = rows.at[p, y]
+            start([remote(mine, mine, a3s.at[p, k], a3r.at[p, k], (d, plus(y, k, NY)))])
+
+    def rows_step(i):
+        if i in AT_Q:
+            rows_q(AT_Q.index(i))
+        if i in AT_Y:
+            rows_y(AT_Y.index(i))
 
     def rows_done():
-        for k in range(1, NY):
-            at = plus(y, -k, NY)
-            arrive([remote(rows.at[at], rows.at[at], a3s.at[k], a3r.at[k], (d, at))])
+        for p in range(PIECES):
+            for k in range(1, NY):
+                at = plus(y, -k, NY)
+                arrive([remote(rows.at[p, at], rows.at[p, at], a3s.at[p, k], a3r.at[p, k], (d, at))])
 
     def transpose_cot():
         keep = r_col >= 0
@@ -220,28 +266,31 @@
         lax.fori_loop(0, NZ * NQ, one, 0)
         ctp[...] = ctp32[...].astype(BF)
 
-    for i in range(NZ + LAGS):
+    for i in range(LAST):
         if i < NZ:
+            ref = chunk(plus(z, ORDER[i], NZ), x, c)
             if i > 0:
-                arrive(move(chunk(plus(z, z_offset(i), NZ), x, c), zs, zr, i, up))
-            send_z(i)
+                arrive(move(ref, zs, zr, i, right))
+            send_z(ref, zs, zr, i)
             send_x(i)
-        if i < 8:
-            for k in (2 * i + 1, 2 * i + 2):
-                if k < NZ:
-                    rows_z(k)
+        if i == 0:
+            down_x()
+        if i == 1:
+            down_x2()
+        rows_z(i)
         if 0 <= i - LAGX < NZ:
             pass_x(i - LAGX)
+        if 0 <= i - LAGD < NZ:
+            down_z(i - LAGD)
         if 0 <= i - LAGS < NZ:
             to_sibling(i - LAGS)
-        if i == 3:
+        if i == TURN:
             transpose_cot()
-        if i == 10:
-            rows_q()
-        if i == 14:
-            rows_y()
+        rows_step(i)
     for i in range(NZ):
-        arrive(move(group(plus(z, z_offset(i), NZ), 1 - c), sbs, sbr, i, sibling))
+        arrive(move(group(plus(z, ORDER[i], NZ), 1 - c), sbs, sbr, i, sibling))
+
+    rows_step(LAST)
 
     def preacts(gate_f32, up_f32):
         gate = gate_f32.astype(BF).astype(F32)
@@ -263,6 +312,8 @@
 
     lax.fori_loop(0, HID // TILE, forward, 0)
 
+    rows_step(LAST + 1)
+
     half = DW // 2
 
     def other_half(m, carry):
@@ -275,6 +326,9 @@
     lax.fori_loop(0, half // TILE, other_half, 0)
     to_other = [remote(p_send, p_recv, p0s.at[0], p0r.at[0], sibling)]
     start(to_other)
+
+    for i in range(NZ):
+        arrive(move(down_group(plus(z, ORDER[i], NZ), 1 - c), dss, dsr, i, sibling))
 
     def layer_part(yy):
         return lax.dot_general(
@@ -291,6 +345,8 @@
         layer_copies.append(remote(l_send.at[k], l_recv.at[k], ls.at[k], lr.at[k], (d, to)))
         start(layer_copies[-1:])
     l_send[0] = layer_part(y)
+
+    rows_step(LAST + 2)
 
     def own_half(m, carry):
         at = pl.multiple_of(c * half + m * TILE, TILE)
@@ -311,6 +367,8 @@
     at = pl.ds(pl.multiple_of(x * 128, 128), 128)
     x_own[...] = p_own[at, :] + p_recv[at, :].astype(F32)
 
+    rows_step(LAST + 3)
+
     rows_done()
 
     def backward(t, carry):
@@ -319,15 +377,12 @@
         up_value = jnp.zeros((TOK, TILE), F32)
         d_hidden = jnp.zeros((TOK, TILE), F32)
         for yy in range(NY):
-            gate += jnp.dot(
-                rows[yy, :, :SQ], w[0, yy * SQ : (yy + 1) * SQ, cols], preferred_element_type=F32
-            )
-            up_value += jnp.dot(
-                rows[yy, :, :SQ], w[1, yy * SQ : (yy + 1) * SQ, cols], preferred_element_type=F32
-            )
-            d_hidden += jnp.dot(
-                rows[yy, :, SQ:], dn[yy * CQ : (yy + 1) * CQ, cols], preferred_element_type=F32
-            )
+            for p in range(2):
+                at = slice(yy * SQ + p * TILE, yy * SQ + (p + 1) * TILE)
+                gate += jnp.dot(rows[p, yy], w[0, at, cols], preferred_element_type=F32)
+                up_value += jnp.dot(rows[p, yy], w[1, at, cols], preferred_element_type=F32)
+            at = slice(yy * CQ, (yy + 1) * CQ)
+            d_hidden += jnp.dot(rows[2, yy], dn[at, cols], preferred_element_type=F32)
         gate, up_value, sig, active = preacts(gate, up_value)
         gates_ref[:, cols] = (d_hidden * up_value * (sig * (1.0 + gate * (1.0 - sig)))).astype(BF)
         linear_ref[:, cols] = (d_hidden * active).astype(BF)
@@ -380,17 +435,23 @@
             jax.ShapeDtypeStruct((TOK, HID), BF),
             jax.ShapeDtypeStruct((DW // 128, HID), F32),
         ),
-        in_specs=[pl.BlockSpec(memory_space=pltpu.VMEM)] * 5,
+        in_specs=[pl.BlockSpec(memory_space=pl.ANY)] * 5,
         out_specs=tuple(pl.BlockSpec(memory_space=pltpu.VMEM) for _ in range(4)),
         scratch_shapes=[
+            vm((1, TOK), jnp.int32),
+            vm((TOK, D)),
+            vm((2, 16, HID)),
+            vm((8, HID)),
+            vm((TOK, DW)),
+            dma(5),
             vm((2, D, HID)),
             vm((DW, HID)),
             vm((8, HID)),
-            vm((NZ, 16, WQ)),
-            vm((NZ, 16, WQ)),
-            vm((NQ, 32, WQ)),
-            vm((NQ, 32, WQ)),
-            vm((NY, TOK, WQ)),
+            vm((PIECES, NZ, 16, TILE)),
+            vm((PIECES, NZ, 16, TILE)),
+            vm((PIECES, NQ, 32, TILE)),
+            vm((PIECES, NQ, 32, TILE)),
+            vm((PIECES, NY, TOK, TILE)),
             vm((TOK, HID)),
             vm((DW, TOK), F32),
             vm((DW, TOK), F32),
@@ -408,11 +469,15 @@
             dma(2),
             dma(2),
         ]
-        + [dma(2, NZ)] * 10
-        + [dma(NZ), dma(NZ), dma(NQ), dma(NQ), dma(NY), dma(NY)]
+        + [dma(NZ)] * 10
+        + [dma(3), dma(3)]
+        + [dma(NZ)] * 4
+        + [dma(PIECES, NZ)] * 2
+        + [dma(PIECES, NQ)] * 2
+        + [dma(PIECES, NY)] * 2
         + [dma(1), dma(1), dma(NX), dma(NX), dma(NZ), dma(NZ), dma(NY), dma(NY)],
         compiler_params=pltpu.CompilerParams(
-            collective_id=0, has_side_effects=True, vmem_limit_bytes=48 * 1024 * 1024
+            collective_id=0, has_side_effects=True, vmem_limit_bytes=60 * 1024 * 1024
         ),
     )(routes.reshape(1, TOK), states, inner_weights, down_weight, cotangent)
 

time: 112 us -> 102 us (0.911)
  the two profiles are of different devices: /device:TPU:1 before, /device:TPU:8 now
where the time goes in v2:
time: 102 us
  Pallas kernels  96.2 us (94%)
  local copies, waits for them, and re-layouts  4.75 us (5%)
    pallas_call x1, Pallas kernels, body(): pl.pallas_call(kernel, out_shape=(jax.ShapeDtypeStruct((TOK, DW // NY), B...  96.2 us
    unnamed x8, local copies, waits for them, and re-layouts  4.75 us

profile of v2, /device:TPU:8, one launch (start us, length us, event | category | flops | bytes accessed | tf_op | source)
XLA Modules:
  0.0 101.6 jit_solution(480385541345133138)
XLA Ops:
  0.6 96.2 %shard_map.84 = (bf16[256,256]{1,0:T(8,128)(2,1)}, bf16[256,768]{1,0:T(8,128)(2,1)}, bf16[256,768]{1,0:T(8,128)(2,1)}, f32[8,768]{1,0:T(8,128)}) custom-call(s32[1,256]{1,0:T(1,128)} %bitcast.1, bf16[256,2048]{1,0:T(8,128)(2,1)} %states_in.1, bf16[2,16,768]{2,1,0:T(8,128)(2,1)} %inner_in.1, bf16[8,768]{1,0:T(8,128)(2,1)} %down_in.1, bf16[256,1024]{1,0:T(8,128)(2,1)} %cot_in.1), custom_call_target="tpu_custom_call" | custom-call | tf_op jit(solution)/shard_map/pallas_call | solution.py:430
  96.8 1.6 %copy.13 = bf16[256,256]{1,0:T(8,128)(2,1)} copy(bf16[256,256]{1,0:T(8,128)(2,1)} %get-tuple-element.8) | data formatting | bytes 262144
  98.4 0.0 copy-start
  98.4 1.8 %copy.14 = bf16[256,768]{1,0:T(8,128)(2,1)} copy(bf16[256,768]{1,0:T(8,128)(2,1)} %get-tuple-element.9) | data formatting | bytes 786432
  100.2 0.0 copy-done
  100.2 0.0 copy-start.1
  100.2 0.7 copy.15
  101.0 0.0 copy-done.1
  101.0 0.6 copy.16
Async XLA Ops:
  98.4 1.8 %copy-start = (bf16[256,768]{1,0:T(8,128)(2,1)S(1)}, bf16[256,768]{1,0:T(8,128)(2,1)}, u32[]{:S(2)}) copy-start(bf16[256,768]{1,0:T(8,128)(2,1)} %get-tuple-element.10) | copy-start | bytes 1179652
  100.2 0.8 copy-start.1

commit v3 on v2

--- a/solution.py
+++ b/solution.py
@@ -33,6 +33,8 @@
 LAGS = 4
 LAGD = 3
 LAST = NZ + 4
+BATCH = 4
+AT_ADD = (10, 14, 18)
 
 
 def goes_right(i):
@@ -45,7 +47,7 @@
     routes_ref, states_ref, inner_ref, down_ref, cot_ref, in_sem,
     w, dn, dsib, s_buf, r1, t_buf, r2, rows, hidden, ct, ctp32, ctp,
     p_send, p_recv, p_own, x_send, x_recv, x_own, z_send, z_recv, l_send, l_recv,
-    sib0_s, sib0_r, zs, zr, xls, xlr, xrs, xrr, x2s, x2r, sbs, sbr, dxs, dxr, dzs, dzr, dss, dsr,
+    acc, sib0_s, sib0_r, zs, zr, xls, xlr, xrs, xrr, x2s, x2r, sbs, sbr, dxs, dxr, dzs, dzr, dss, dsr,
     a1s, a1r, a2s, a2r, a3s, a3r, p0s, p0r, p1s, p1r, p2s, p2r, ls, lr,
 ):
     d, y = lax.axis_index("dp"), lax.axis_index("mp")
@@ -238,6 +240,35 @@
         for k in range(1, NY):
             mine = rows.at[p, y]
             start([remote(mine, mine, a3s.at[p, k], a3r.at[p, k], (d, plus(y, k, NY)))])
+
+    def columns(t):
+        if isinstance(t, int):
+            return slice(t * TILE, (t + 1) * TILE)
+        return pl.ds(pl.multiple_of(t * TILE, TILE), TILE)
+
+    def group_product(n, lane, cols):
+        total = None
+        for i in range(n * BATCH, (n + 1) * BATCH):
+            at = pl.ds(pl.multiple_of(plus(z, ORDER[i], NZ) * 128, 128), 128)
+            one = jnp.dot(states_ref[:, at], w[lane, at, cols], preferred_element_type=F32)
+            total = one if total is None else total + one
+        return total
+
+    def groups_arrive(n):
+        for i in range(n * BATCH, (n + 1) * BATCH):
+            arrive(move(group(plus(z, ORDER[i], NZ), 1 - c), sbs, sbr, i, sibling))
+
+    def add_groups(n):
+        groups_arrive(n)
+
+        def one(t, carry):
+            cols = columns(t)
+            for lane in range(2):
+                more = group_product(n, lane, cols)
+                acc[lane, :, cols] = more if n == 0 else acc[lane, :, cols] + more
+            return carry
+
+        lax.fori_loop(0, HID // TILE, one, 0)
 
     def rows_step(i):
         if i in AT_Q:
@@ -287,8 +318,9 @@
         if i == TURN:
             transpose_cot()
         rows_step(i)
-    for i in range(NZ):
-        arrive(move(group(plus(z, ORDER[i], NZ), 1 - c), sbs, sbr, i, sibling))
+        if i in AT_ADD:
+            add_groups(AT_ADD.index(i))
+    groups_arrive(NZ // BATCH - 1)
 
     rows_step(LAST)
 
@@ -298,34 +330,65 @@
         sig = jax.nn.sigmoid(gate)
         return gate, up_value, sig, gate * sig
 
-    def columns(t):
-        return pl.ds(pl.multiple_of(t * TILE, TILE), TILE)
-
     def forward(t, carry):
         cols = columns(t)
         _, up_value, _, active = preacts(
-            jnp.dot(states_ref[...], w[0, :, cols], preferred_element_type=F32),
-            jnp.dot(states_ref[...], w[1, :, cols], preferred_element_type=F32),
+            acc[0, :, cols] + group_product(NZ // BATCH - 1, 0, cols),
+            acc[1, :, cols] + group_product(NZ // BATCH - 1, 1, cols),
         )
         hidden[:, cols] = (active * up_value).astype(BF)
         return carry
 
-    lax.fori_loop(0, HID // TILE, forward, 0)
-
+    half = DW // 2
+    tiles = range(HID // TILE)
+
+    def product(t, first_row, m):
+        at = pl.multiple_of(first_row + m * TILE, TILE)
+        return jnp.dot(ctp[pl.ds(at, TILE), :], hidden[:, columns(t)], preferred_element_type=F32)
+
+    def core_send(t):
+        for m in range(half // TILE):
+            p_send[t, m * TILE : (m + 1) * TILE, :] = product(t, (1 - c) * half, m).astype(BF)
+        start([remote(p_send.at[t], p_recv.at[t], p0s.at[t], p0r.at[t], sibling)])
+        for m in range(half // TILE):
+            p_own[t, m * TILE : (m + 1) * TILE, :] = product(t, c * half, m)
+
+    def x_copy(t, k):
+        to = dev(z, plus(x, k, NX), c)
+        return remote(x_send.at[t, k], x_recv.at[t, k], p1s.at[t, k], p1r.at[t, k], to)
+
+    def x_sends(t):
+        arrive([remote(p_send.at[t], p_recv.at[t], p0s.at[t], p0r.at[t], sibling)])
+        for k in (2, 1, 3):
+            at = pl.ds(pl.multiple_of(plus(x, k, NX) * 128, 128), 128)
+            x_send[t, k] = (p_own[t, at, :] + p_recv[t, at, :].astype(F32)).astype(BF)
+            start([x_copy(t, k)])
+        at = pl.ds(pl.multiple_of(x * 128, 128), 128)
+        x_own[t] = p_own[t, at, :] + p_recv[t, at, :].astype(F32)
+
+    def z_copy(t, k):
+        to = plus(z, k, NZ)
+        return remote(z_send.at[t, to], z_recv.at[t, k], p2s.at[t, k], p2r.at[t, k], dev(to, x, c))
+
+    def z_sends(t):
+        arrive([x_copy(t, k) for k in range(1, NX)])
+        total = x_own[t]
+        for k in range(1, NX):
+            total += x_recv[t, k].astype(F32)
+        x_own[t] = total
+        pieces = total.reshape(NZ, 8, TILE)
+        z_send[t] = jnp.concatenate([pieces[:, :, :128], pieces[:, :, 128:]], axis=1).astype(BF)
+        start([z_copy(t, k) for k in FAR])
+
+    forward(0, 0)
+    core_send(0)
+    forward(1, 0)
+    core_send(1)
+    x_sends(0)
     rows_step(LAST + 1)
-
-    half = DW // 2
-
-    def other_half(m, carry):
-        at = pl.multiple_of((1 - c) * half + m * TILE, TILE)
-        p_send[pl.ds(pl.multiple_of(m * TILE, TILE), TILE), :] = jnp.dot(
-            ctp[pl.ds(at, TILE), :], hidden[...], preferred_element_type=F32
-        ).astype(BF)
-        return carry
-
-    lax.fori_loop(0, half // TILE, other_half, 0)
-    to_other = [remote(p_send, p_recv, p0s.at[0], p0r.at[0], sibling)]
-    start(to_other)
+    forward(2, 0)
+    core_send(2)
+    x_sends(1)
 
     for i in range(NZ):
         arrive(move(down_group(plus(z, ORDER[i], NZ), 1 - c), dss, dsr, i, sibling))
@@ -338,36 +401,20 @@
             preferred_element_type=F32,
         ).astype(BF)
 
+    x_sends(2)
     layer_copies = []
     for k in range(1, NY):
         to = plus(y, k, NY)
         l_send[k] = layer_part(to)
         layer_copies.append(remote(l_send.at[k], l_recv.at[k], ls.at[k], lr.at[k], (d, to)))
         start(layer_copies[-1:])
+    rows_step(LAST + 2)
+    z_sends(0)
     l_send[0] = layer_part(y)
-
-    rows_step(LAST + 2)
-
-    def own_half(m, carry):
-        at = pl.multiple_of(c * half + m * TILE, TILE)
-        p_own[pl.ds(pl.multiple_of(m * TILE, TILE), TILE), :] = jnp.dot(
-            ctp[pl.ds(at, TILE), :], hidden[...], preferred_element_type=F32
-        )
-        return carry
-
-    lax.fori_loop(0, half // TILE, own_half, 0)
-    arrive(to_other)
-    x_copies = []
-    for k in range(1, NX):
-        to = plus(x, k, NX)
-        at = pl.ds(pl.multiple_of(to * 128, 128), 128)
-        x_send[k] = (p_own[at, :] + p_recv[at, :].astype(F32)).astype(BF)
-        x_copies.append(remote(x_send.at[k], x_recv.at[k], p1s.at[k], p1r.at[k], dev(z, to, c)))
-        start(x_copies[-1:])
-    at = pl.ds(pl.multiple_of(x * 128, 128), 128)
-    x_own[...] = p_own[at, :] + p_recv[at, :].astype(F32)
-
     rows_step(LAST + 3)
+    z_sends(1)
+    z_sends(2)
+    rows_step(LAST + 4)
 
     rows_done()
 
@@ -388,21 +435,7 @@
         linear_ref[:, cols] = (d_hidden * active).astype(BF)
         return carry
 
-    lax.fori_loop(0, 1, backward, 0)
-
-    arrive(x_copies)
-    x_own[...] = (
-        x_own[...] + x_recv[1].astype(F32) + x_recv[2].astype(F32) + x_recv[3].astype(F32)
-    )
-    z_copies = []
-    for k in range(1, NZ):
-        to = plus(z, k, NZ)
-        piece = x_own[pl.ds(pl.multiple_of(to * 8, 8), 8), :]
-        z_send[k] = jnp.concatenate([piece[:, :384], piece[:, 384:]], axis=0).astype(BF)
-        z_copies.append(remote(z_send.at[k], z_recv.at[k], p2s.at[k], p2r.at[k], dev(to, x, c)))
-        start(z_copies[-1:])
-
-    lax.fori_loop(1, HID // TILE, backward, 0)
+    lax.fori_loop(0, HID // TILE, backward, 0)
 
     arrive(layer_copies)
     layer_ref[...] = (
@@ -412,13 +445,14 @@
         + l_recv[3].astype(F32)
     ).astype(BF)
 
-    arrive(z_copies)
-    total = z_recv[1].astype(F32)
-    for k in range(2, NZ):
-        total += z_recv[k].astype(F32)
-    mine = x_own[pl.ds(pl.multiple_of(z * 8, 8), 8), :]
-    dgrad_ref[:, :384] = mine[:, :384] + total[:8]
-    dgrad_ref[:, 384:] = mine[:, 384:] + total[8:]
+    for t in tiles:
+        arrive([z_copy(t, k) for k in FAR])
+        total = z_recv[t, 1].astype(F32)
+        for k in range(2, NZ):
+            total += z_recv[t, k].astype(F32)
+        mine = x_own[t, pl.ds(pl.multiple_of(z * 8, 8), 8), :]
+        dgrad_ref[:, t * TILE : t * TILE + 128] = mine[:, :128] + total[:8]
+        dgrad_ref[:, t * TILE + 128 : (t + 1) * TILE] = mine[:, 128:] + total[8:]
 
     for one in sends:
         one.wait_send()
@@ -456,16 +490,17 @@
             vm((DW, TOK), F32),
             vm((DW, TOK), F32),
             vm((DW, TOK)),
-            vm((DW // 2, HID)),
-            vm((DW // 2, HID)),
-            vm((DW // 2, HID), F32),
-            vm((NX, 128, HID)),
-            vm((NX, 128, HID)),
-            vm((128, HID), F32),
-            vm((NZ, 16, HID // 2)),
-            vm((NZ, 16, HID // 2)),
+            vm((HID // TILE, DW // 2, TILE)),
+            vm((HID // TILE, DW // 2, TILE)),
+            vm((HID // TILE, DW // 2, TILE), F32),
+            vm((HID // TILE, NX, 128, TILE)),
+            vm((HID // TILE, NX, 128, TILE)),
+            vm((HID // TILE, 128, TILE), F32),
+            vm((HID // TILE, NZ, 16, 128)),
+            vm((HID // TILE, NZ, 16, 128)),
             vm((NY, TOK, DW // NY)),
             vm((NY, TOK, DW // NY)),
+            vm((2, TOK, HID), F32),
             dma(2),
             dma(2),
         ]
@@ -475,7 +510,7 @@
         + [dma(PIECES, NZ)] * 2
         + [dma(PIECES, NQ)] * 2
         + [dma(PIECES, NY)] * 2
-        + [dma(1), dma(1), dma(NX), dma(NX), dma(NZ), dma(NZ), dma(NY), dma(NY)],
+        + [dma(3), dma(3), dma(3, NX), dma(3, NX), dma(3, NZ), dma(3, NZ), dma(NY), dma(NY)],
         compiler_params=pltpu.CompilerParams(
             collective_id=0, has_side_effects=True, vmem_limit_bytes=60 * 1024 * 1024
         ),

time: 102 us -> 97.1 us (0.952)
  the two profiles are of different devices: /device:TPU:8 before, /device:TPU:1 now
where the time goes in v3:
time: 97.1 us; the launch traced here: 96.9 us
  Pallas kernels  91.5 us (94%)
  local copies, waits for them, and re-layouts  4.75 us (5%)
    pallas_call x1, Pallas kernels, body(): pl.pallas_call(kernel, out_shape=(jax.ShapeDtypeStruct((TOK, DW // NY), B...  91.5 us
    unnamed x8, local copies, waits for them, and re-layouts  4.75 us

profile of v3, /device:TPU:1, one launch (start us, length us, event | category | flops | bytes accessed | tf_op | source)
XLA Modules:
  0.0 96.9 jit_solution(18392495306107484353)
XLA Ops:
  0.6 91.5 %shard_map.84 = (bf16[256,256]{1,0:T(8,128)(2,1)}, bf16[256,768]{1,0:T(8,128)(2,1)}, bf16[256,768]{1,0:T(8,128)(2,1)}, f32[8,768]{1,0:T(8,128)}) custom-call(s32[1,256]{1,0:T(1,128)} %bitcast.1, bf16[256,2048]{1,0:T(8,128)(2,1)} %states_in.1, bf16[2,16,768]{2,1,0:T(8,128)(2,1)} %inner_in.1, bf16[8,768]{1,0:T(8,128)(2,1)} %down_in.1, bf16[256,1024]{1,0:T(8,128)(2,1)} %cot_in.1), custom_call_target="tpu_custom_call" | custom-call | tf_op jit(solution)/shard_map/pallas_call | solution.py:464
  92.1 1.6 %copy.13 = bf16[256,256]{1,0:T(8,128)(2,1)} copy(bf16[256,256]{1,0:T(8,128)(2,1)} %get-tuple-element.8) | data formatting | bytes 262144
  93.7 0.0 copy-start
  93.7 1.8 %copy.14 = bf16[256,768]{1,0:T(8,128)(2,1)} copy(bf16[256,768]{1,0:T(8,128)(2,1)} %get-tuple-element.9) | data formatting | bytes 786432
  95.5 0.0 copy-done
  95.5 0.0 copy-start.1
  95.5 0.7 copy.15
  96.2 0.0 copy-done.1
  96.2 0.6 copy.16
Async XLA Ops:
  93.7 1.8 %copy-start = (bf16[256,768]{1,0:T(8,128)(2,1)S(1)}, bf16[256,768]{1,0:T(8,128)(2,1)}, u32[]{:S(2)}) copy-start(bf16[256,768]{1,0:T(8,128)(2,1)} %get-tuple-element.10) | copy-start | bytes 1179652
  95.5 0.8 copy-start.1
